TPU v7x, 32 devices: a whole 2x2x4 slice. The times are simulated.
32 devices in a mesh: tile: 8 (over y, x, core), chan: 4 (over z).
Axes of the slice: x: 2, y: 2, z: 4, core: 2. Of those that a mesh axis runs over, the one named last changes fastest.
Arguments:
- points: bfloat16 [128, 8192], P('chan', 'tile'), may hold values from -6 to 6
- dest: int32 [8192, 1], P('tile'), may hold values from 0 to 7; in each aligned block of 1024 rows (0 to 1023, 1024 to 2047, ...) at most 384 rows name the same one
- voxel: int32 [8192, 1], P('tile'), may hold values from 0 to 2047
- weight: bfloat16 [256, 27, 128], P('chan'), may hold values from -0.109375 to 0.109375
- grad_out: bfloat16 [256, 16384], P('chan', 'tile'), may hold values from -6 to 6
Outputs:
- features_out: bfloat16 [256, 16384], P('chan', 'tile')
- weight_grad: float32 [256, 3456], P('chan', 'tile')
Inputs may be any that keep to these rules, and one draw needn't show every extreme that they name: `dest`: among the 1024 points of one scene owner (aligned blocks of rows), at most 384 go to any one tile, and some tile receives exactly 384 of them.
All inputs are finite; a program needn't handle non-finite values.
Results may differ from a plain program's by a relative error of at most 0.0029.
Values may be sent and summed in bfloat16 or wider, within the bound.
A program may use at most 64 MiB of HBM per device.

v0:
```python
import jax
import jax.numpy as jnp
from jax import lax
from jax.sharding import PartitionSpec as P

C_IN = 128
EDGE = 16
DEPTH = 8
VOX = 2048


def tile_conv(grid_part, weight_part, masked):
    count = grid_part.shape[0]
    cube = grid_part.reshape(count, DEPTH, EDGE, EDGE)
    padded = jnp.pad(cube, ((0, 0), (1, 1), (1, 1), (1, 1)))
    stacked = []
    for index in range(27):
        first, second, third = (index // 9, index // 3 % 3, index % 3)
        stacked.append(
            padded[:, first : first + DEPTH, second : second + EDGE, third : third + EDGE].reshape(
                count, DEPTH * EDGE * EDGE
            )
        )
    columns = jnp.stack(stacked, axis=0).reshape(27 * count, DEPTH * EDGE * EDGE)
    out_rows = weight_part.shape[0]
    output = jnp.dot(
        weight_part.reshape(out_rows, 27 * count), columns, preferred_element_type=jnp.float32
    )
    grads = lax.dot_general(
        masked, columns, (((1,), (1,)), ((), ())), preferred_element_type=jnp.float32
    )
    return (output, grads.reshape(out_rows, 27, count))


def voxelize(features, cells):
    sums = (
        jnp.zeros((features.shape[0], VOX), jnp.float32)
        .at[:, cells]
        .add(features.astype(jnp.float32), mode="drop")
    )
    counts = jnp.zeros((VOX,), jnp.float32).at[cells].add(1.0, mode="drop")
    grid = (sums / jnp.maximum(counts, 1.0)[None, :]).astype(jnp.bfloat16)
    return (grid, (counts > 0).astype(jnp.float32))


def pack_rows(features, place, voxel, slots):
    send = jnp.zeros((features.shape[0], slots), jnp.bfloat16).at[:, place].set(features)
    cells = jnp.full((1, slots), VOX, jnp.int32).at[0, place].set(voxel[:, 0])
    return (send, cells)


def on_device(points, dest, voxel, weight, grad_out):
    tiles = lax.axis_size("tile")
    count = dest.shape[0]
    capacity = min(count, 3 * count // tiles)
    onehot = (dest == jnp.arange(tiles, dtype=jnp.int32)[None, :]).astype(jnp.int32)
    before = jnp.cumsum(onehot, axis=0) - onehot
    place = dest[:, 0] * capacity + jnp.sum(before * onehot, axis=1)
    slots = tiles * capacity
    out_rows = weight.shape[0]
    all_channels = lax.all_gather(points, "chan", axis=0, tiled=True)
    send, cells = pack_rows(all_channels, place, voxel, slots)
    received, got_cells = (
        lax.all_to_all(send, "tile", split_axis=1, concat_axis=1, tiled=True),
        lax.all_to_all(cells, "tile", split_axis=1, concat_axis=1, tiled=True),
    )
    grid, occupied = voxelize(received, got_cells[0])
    masked = (grad_out.astype(jnp.float32) * occupied[None, :]).astype(jnp.bfloat16)
    partial_out, partial_grads = tile_conv(grid, weight, masked)
    grads = partial_grads
    output, grads = (partial_out, grads)
    features_out = (output * occupied[None, :]).astype(jnp.bfloat16)
    weight_grad = lax.psum_scatter(
        grads.reshape(out_rows, 27 * C_IN), "tile", scatter_dimension=1, tiled=True
    )
    return (features_out, weight_grad)


def solution(mesh):
    placed = (
        P("chan", "tile"),
        P("tile", None),
        P("tile", None),
        P("chan", None, None),
        P("chan", "tile"),
    )
    return jax.shard_map(
        on_device,
        mesh=mesh,
        in_specs=placed,
        out_specs=(P("chan", "tile"), P("chan", "tile")),
        check_vma=False,
    )
```

profile of v0, /device:TPU:1, one launch (start us, length us, event | category | flops | bytes accessed | tf_op | source)
XLA Modules:
  0.0 213.7 jit_solution(5327839853387718878)
XLA Ops:
  7.2 0.7 fusion.11
  7.9 2.3 %reduce-window.6 = s32[8,8,128]{2,1,0:T(8,128)S(1)} reduce-window(s32[8,8,128]{2,1,0:T(8,128)S(1)} %fusion.11, s32[]{:T(128)} %constant.10.clone.1), window={size=1x1x128 pad=0_0x0_0x127_0}, to_apply=%region_0.0 | reduce-window | flops 1040384 | bytes 65540 | tf_op jit(solution)/shard_map/reduce-window
  10.2 0.3 slice_reduce_fusion
  10.5 0.2 reduce-window.9
  10.7 0.7 fusion.10
  11.4 0.7 compare_select_fusion.1
  12.1 0.7 and_reduce_fusion
  12.9 0.7 fusion.12
  13.6 5.0 %scatter_custom_fusion.3 = s32[3072]{0:T(1024)} fusion(s32[1024]{0:T(1024)S(1)} %broadcast_select_fusion, s32[1024]{0:T(1024)} %bitcast.122, s32[]{:T(128)} %constant.8.clone.1), kind=kCustom, calls=%fused_computation.85 | custom fusion | bytes 12800
  18.7 5.2 %all-to-all-start = ((s32[1,8,384]{2,0,1:T(1,128)}), s32[1,8,384]{2,0,1:T(1,128)S(1)}, u32[]{:S(2)}, u32[]{:S(2)}) async-start(s32[1,8,384]{2,0,1:T(1,128)} %bitcast.5), calls=%async_computation | async-start | bytes 24576 | tf_op jit(solution)/shard_map/all_to_all | solution.py:65
  23.9 12.4 %all_gather.3 = bf16[128,1024]{1,0:T(8,128)(2,1)S(1)} all-gather(bf16[32,1024]{1,0:T(8,128)(2,1)} %param.5), channel_id=1, replica_groups=mesh['tile'=8,'chan'=4] {'chan'}, dimensions={0}, use_global_device_ids=true | all-gather | bytes 327680 | tf_op jit(solution)/shard_map/all_gather | solution.py:61
  36.3 0.2 copy.38
  36.5 4.1 %scatter_custom_fusion = bf16[128,3072]{0,1:T(8,128)(2,1)} fusion(s32[1024]{0:T(1024)S(1)} %bitcast.117, bf16[1024,128]{1,0:T(8,128)(2,1)S(1)} %copy.38, bf16[]{:T(256)} %constant.12.clone.1), kind=kCustom, calls=%fused_computation.41 | custom fusion | bytes 786434 | tf_op jit(solution)/shard_map/scatter | solution.py:47
  40.6 6.0 %all-to-all-start.1 = ((bf16[128,8,384]{0,2,1:T(8,128)(2,1)}), bf16[128,8,384]{0,2,1:T(8,128)(2,1)S(1)}, u32[]{:S(2)}, u32[]{:S(2)}) async-start(bf16[128,8,384]{0,2,1:T(8,128)(2,1)} %bitcast.10), calls=%async_computation.1 | async-start | bytes 1572864 | tf_op jit(solution)/shard_map/all_to_all | solution.py:64
  46.7 16.6 %scatter_custom_fusion.2 = f32[2048]{0:T(1024)S(1)} fusion(s32[3072]{0:T(1024)S(1)} %bitcast.120, f32[3072]{0:T(1024)S(1)} %broadcast.68, f32[]{:T(128)} %constant.7.clone.1), kind=kCustom, calls=%fused_computation.88 | custom fusion | flops 3072 | bytes 8196 | tf_op jit(solution)/shard_map/scatter-add | solution.py:41
  63.3 17.2 %scatter_custom_fusion.1 = f32[128,2048]{0,1:T(8,128)S(1)} fusion(s32[3072]{0:T(1024)S(1)} %bitcast.121, bf16[128,3072]{0,1:T(8,128)(2,1)S(1)} %bitcast.85, f32[]{:T(128)} %constant.7.clone.1), kind=kCustom, calls=%fused_computation.36 | custom fusion | flops 786432 | bytes 1835012 | tf_op jit(solution)/shard_map/scatter-add | solution.py:39
  80.5 0.3 copy.39
  80.9 0.3 copy.40
  81.2 2.1 pad_slice_fusion.1
  83.3 4.4 %pad_slice_fusion = (bf16[128,8,16,16]{0,3,2,1:T(8,128)(2,1)}, bf16[128,8,16,16]{0,3,2,1:T(8,128)(2,1)}, bf16[128,8,16,16]{0,3,2,1:T(8,128)(2,1)}, bf16[128,8,16...) fusion(bf16[128,8,16,16]{0,3,2,1:T(8,128)(2,1)S(1)} %bitcast.84), kind=kLoop, calls=%fused_computation.4 | loop fusion | bytes 10485760 | tf_op jit(solution)/shard_map/slice | solution.py:20
  87.7 2.1 copy.65
  89.8 2.1 copy.60
  91.8 2.1 copy.61
  93.9 2.1 copy.62
  96.0 2.0 copy.63
  98.0 2.1 copy.64
  100.1 2.1 copy.41
  102.2 2.0 copy.66
  104.2 2.0 copy.42
  106.3 2.1 copy.43
  108.3 2.1 copy.44
  110.4 2.1 copy.45
  112.4 2.1 copy.46
  114.5 2.0 copy.47
  116.6 2.0 copy.48
  118.6 2.1 copy.49
  120.7 2.1 copy.50
  122.8 2.0 copy.51
  124.8 2.1 copy.52
  126.9 2.1 copy.53
  128.9 2.1 copy.54
  131.0 2.1 copy.55
  133.0 2.1 copy.56
  135.1 1.0 copy.57
  136.1 1.0 copy.58
  137.1 1.1 copy.59
  138.3 1.2 constant_dynamic-update-slice_fusion.25
  139.5 1.7 constant_dynamic-update-slice_fusion.24
  141.2 1.1 constant_dynamic-update-slice_fusion.23
  142.3 1.1 constant_dynamic-update-slice_fusion.22
  143.3 1.1 constant_dynamic-update-slice_fusion.21
  144.4 1.1 constant_dynamic-update-slice_fusion.20
  145.5 1.1 constant_dynamic-update-slice_fusion.19
  146.6 1.1 constant_dynamic-update-slice_fusion.18
  147.7 1.1 constant_dynamic-update-slice_fusion.17
  148.7 1.1 constant_dynamic-update-slice_fusion.16
  149.8 1.1 constant_dynamic-update-slice_fusion.15
  150.9 1.1 constant_dynamic-update-slice_fusion.14
  152.0 1.1 constant_dynamic-update-slice_fusion.13
  153.9 5.0 %copy-done.1 = bf16[27,128,2048]{2,1,0:T(8,128)(2,1)} copy-done((bf16[27,128,2048]{2,1,0:T(8,128)(2,1)}, bf16[27,128,2048]{2,1,0:T(8,128)(2,1)S(1)}, u32[]{:S(2)}) %copy-start.1) | copy-done | bytes 14155800
  159.0 5.2 %convolution_bitcast_fusion = f32[3456,64]{1,0:T(8,128)} fusion(bf16[3456,2048]{1,0:T(8,128)(2,1)S(1)} %bitcast.82, bf16[64,2048]{1,0:T(8,128)(2,1)S(1)} %copy-done.16, f32[2048]{0:T(1024)S(1)} %compare_convert_fusion), kind=kOutput, calls=%fused_computation.30 | convolution fusion | flops 906362880 | bytes 15310848
  164.2 7.2 %fusion.2 = bf16[64,2048]{1,0:T(8,128)(2,1)} fusion(bf16[64,27,128]{2,0,1:T(8,128)(2,1)S(1)} %copy-done, bf16[27,128,2048]{2,1,0:T(8,128)(2,1)} %copy-done.1, f32[2048]{0:T(1024)S(1)} %compare_convert_fusion), kind=kOutput, calls=%fused_computation.34 | convolution fusion | flops 906231808 | bytes 14868480 | tf_op jit(solution)/shard_map/dot_general | solution.py:26
  171.4 33.8 %reduce-scatter.4.cloned.1.call-done = f32[432,64]{1,0:T(8,128)} async-done(((f32[3456,64]{1,0:T(8,128)}), f32[432,64]{1,0:T(8,128)}) %reduce-scatter.4.cloned.1.call-update) | async-done | bytes 110608
  205.1 1.7 copy.68
  (58 shorter events, 0.9 us)
Async XLA Ops:
  7.2 157.0 %copy-start = (bf16[64,27,128]{2,0,1:T(8,128)(2,1)S(1)}, bf16[64,27,128]{2,0,1:T(8,128)(2,1)}, u32[]{:S(2)}) copy-start(bf16[64,27,128]{2,0,1:T(8,128)(2,1)} %param.8) | copy-start | bytes 1327108
  18.7 22.0 %all-to-all-start = ((s32[1,8,384]{2,0,1:T(1,128)}), s32[1,8,384]{2,0,1:T(1,128)S(1)}, u32[]{:S(2)}, u32[]{:S(2)}) async-start(s32[1,8,384]{2,0,1:T(1,128)} %bitcast.5), calls=%async_computation | async-start | bytes 24576 | tf_op jit(solution)/shard_map/all_to_all | solution.py:65
  40.6 22.7 %all-to-all-start.1 = ((bf16[128,8,384]{0,2,1:T(8,128)(2,1)}), bf16[128,8,384]{0,2,1:T(8,128)(2,1)S(1)}, u32[]{:S(2)}, u32[]{:S(2)}) async-start(bf16[128,8,384]{0,2,1:T(8,128)(2,1)} %bitcast.10), calls=%async_computation.1 | async-start | bytes 1572864 | tf_op jit(solution)/shard_map/all_to_all | solution.py:64
  46.6 158.5 %reduce-scatter.4.cloned.1.call-start = ((), (), s32[]{:S(2)}) async-start(), calls=%async_computation.3 | async-start | bytes 1990656
  87.7 47.4 %copy-start.2 = (bf16[128,8,16,16]{0,3,2,1:T(8,128)(2,1)S(1)}, bf16[128,8,16,16]{0,3,2,1:T(8,128)(2,1)}, u32[]{:S(2)}) copy-start(bf16[128,8,16,16]{0,3,2,1:T(8,128)(2,1)} %get-tuple-element.18) | copy-start | bytes 1572868
  136.1 17.7 %copy-start.5 = (bf16[1,128,2048]{2,1,0:T(8,128)(2,1)S(1)}, bf16[1,128,2048]{2,1,0:T(8,128)(2,1)}, u32[]{:S(2)}) copy-start(bf16[1,128,2048]{2,1,0:T(8,128)(2,1)} %copy.64) | copy-start | bytes 1572868
  137.1 16.7 %copy-start.3 = (bf16[1,128,2048]{2,1,0:T(8,128)(2,1)S(1)}, bf16[1,128,2048]{2,1,0:T(8,128)(2,1)}, u32[]{:S(2)}) copy-start(bf16[1,128,2048]{2,1,0:T(8,128)(2,1)} %copy.65) | copy-start | bytes 1572868
  138.2 15.0 %copy-start.15 = (bf16[1,128,2048]{2,1,0:T(8,128)(2,1)S(1)}, bf16[1,128,2048]{2,1,0:T(8,128)(2,1)}, u32[]{:S(2)}) copy-start(bf16[1,128,2048]{2,1,0:T(8,128)(2,1)} %copy.54) | copy-start | bytes 1572868
  138.2 15.0 %copy-start.14 = (bf16[1,128,2048]{2,1,0:T(8,128)(2,1)S(1)}, bf16[1,128,2048]{2,1,0:T(8,128)(2,1)}, u32[]{:S(2)}) copy-start(bf16[1,128,2048]{2,1,0:T(8,128)(2,1)} %copy.55) | copy-start | bytes 1572868
  138.2 15.1 %copy-start.13 = (bf16[1,128,2048]{2,1,0:T(8,128)(2,1)S(1)}, bf16[1,128,2048]{2,1,0:T(8,128)(2,1)}, u32[]{:S(2)}) copy-start(bf16[1,128,2048]{2,1,0:T(8,128)(2,1)} %copy.56) | copy-start | bytes 1572868
  138.2 15.2 %copy-start.12 = (bf16[1,128,2048]{2,1,0:T(8,128)(2,1)S(1)}, bf16[1,128,2048]{2,1,0:T(8,128)(2,1)}, u32[]{:S(2)}) copy-start(bf16[1,128,2048]{2,1,0:T(8,128)(2,1)} %copy.57) | copy-start | bytes 1572868
  138.2 15.2 %copy-start.10 = (bf16[1,128,2048]{2,1,0:T(8,128)(2,1)S(1)}, bf16[1,128,2048]{2,1,0:T(8,128)(2,1)}, u32[]{:S(2)}) copy-start(bf16[1,128,2048]{2,1,0:T(8,128)(2,1)} %copy.58) | copy-start | bytes 1572868
  138.2 15.3 %copy-start.11 = (bf16[1,128,2048]{2,1,0:T(8,128)(2,1)S(1)}, bf16[1,128,2048]{2,1,0:T(8,128)(2,1)}, u32[]{:S(2)}) copy-start(bf16[1,128,2048]{2,1,0:T(8,128)(2,1)} %copy.59) | copy-start | bytes 1572868
  138.2 15.3 %copy-start.9 = (bf16[1,128,2048]{2,1,0:T(8,128)(2,1)S(1)}, bf16[1,128,2048]{2,1,0:T(8,128)(2,1)}, u32[]{:S(2)}) copy-start(bf16[1,128,2048]{2,1,0:T(8,128)(2,1)} %copy.60) | copy-start | bytes 1572868
  138.2 15.4 %copy-start.8 = (bf16[1,128,2048]{2,1,0:T(8,128)(2,1)S(1)}, bf16[1,128,2048]{2,1,0:T(8,128)(2,1)}, u32[]{:S(2)}) copy-start(bf16[1,128,2048]{2,1,0:T(8,128)(2,1)} %copy.61) | copy-start | bytes 1572868
  138.2 15.4 %copy-start.7 = (bf16[1,128,2048]{2,1,0:T(8,128)(2,1)S(1)}, bf16[1,128,2048]{2,1,0:T(8,128)(2,1)}, u32[]{:S(2)}) copy-start(bf16[1,128,2048]{2,1,0:T(8,128)(2,1)} %copy.62) | copy-start | bytes 1572868
  138.3 15.5 %copy-start.6 = (bf16[1,128,2048]{2,1,0:T(8,128)(2,1)S(1)}, bf16[1,128,2048]{2,1,0:T(8,128)(2,1)}, u32[]{:S(2)}) copy-start(bf16[1,128,2048]{2,1,0:T(8,128)(2,1)} %copy.63) | copy-start | bytes 1572868
  138.3 15.6 %copy-start.4 = (bf16[1,128,2048]{2,1,0:T(8,128)(2,1)S(1)}, bf16[1,128,2048]{2,1,0:T(8,128)(2,1)}, u32[]{:S(2)}) copy-start(bf16[1,128,2048]{2,1,0:T(8,128)(2,1)} %copy.66) | copy-start | bytes 1572868
  139.5 19.5 %copy-start.16 = (bf16[64,2048]{1,0:T(8,128)(2,1)S(1)}, bf16[64,2048]{1,0:T(8,128)(2,1)}, u32[]{:S(2)}) copy-start(bf16[64,2048]{1,0:T(8,128)(2,1)} %param.9) | copy-start | bytes 786436
  153.9 5.1 %copy-start.1 = (bf16[27,128,2048]{2,1,0:T(8,128)(2,1)}, bf16[27,128,2048]{2,1,0:T(8,128)(2,1)S(1)}, u32[]{:S(2)}) copy-start(bf16[27,128,2048]{2,1,0:T(8,128)(2,1)S(1)} %constant_dynamic-update-slice_fusion) | copy-start | bytes 42467332
Sparse Core Ops, SparseCore 0:
  164.3 40.7 reduce-scatter.3
where the time goes:
time: 216 us; the launch traced here: 214 us
  local copies, waits for them, and re-layouts  89.2 us (41%)
  other arithmetic  40.1 us (19%)
  waiting for transfers between devices  33.8 us (16%)
  between operations  14.5 us (7%)
  blocking collectives  12.4 us (6%)
  matrix products  12.3 us (6%)
  starting transfers between devices  11.2 us (5%)
    another operation x27, local copies, waits for them, and re-layouts, tile_conv(): jnp.stack(stacked, axis=0).reshape(27 * count, DEPTH * EDGE * EDGE)  50.5 us
    unnamed x2, waiting for transfers between devices  33.8 us
    unnamed x61, local copies, waits for them, and re-layouts  27.1 us
    scatter-add x1, other arithmetic, voxelize(): sums = jnp.zeros((features.shape[0], VOX), jnp.float32).at[:, cells].add(...  17.2 us
    scatter-add x1, other arithmetic, voxelize(): counts = jnp.zeros((VOX,), jnp.float32).at[cells].add(1.0, mode='drop')  16.6 us
    all_gather x1, blocking collectives, on_device(): all_channels = lax.all_gather(points, 'chan', axis=0, tiled=True)  12.4 us
    dot_general x1, matrix products, tile_conv(): jnp.dot(weight_part.reshape(out_rows, 27 * count), columns, preferred_ele...  7.15 us
    slice x2, local copies, waits for them, and re-layouts, tile_conv(): padded[:, first:first + DEPTH, second:second + EDGE, third:third + EDGE]  6.44 us
  transfers between devices with their start and end apart: 3, of which 1 were waited for; matrix products, arithmetic and copies ran while one was open for 13% of the time, Pallas kernels for 0%

commit v1 on v0

v1 whole, which is shorter than its diff:
```python
import functools

import jax
import jax.numpy as jnp
from jax import lax
from jax.experimental import pallas as pl
from jax.experimental.pallas import tpu as pltpu
from jax.sharding import PartitionSpec as P

EDGE = 16
DEPTH = 8
PLANE = EDGE * EDGE
VOX = DEPTH * PLANE
PADDED = PLANE + 2 * EDGE
CHUNKS = 4
PER_CHUNK = DEPTH // CHUNKS
ROWS_MAJOR = (((1,), (1,)), ((), ()))


def repeat(start, stop, body):
    if stop - start <= 8:
        for step in range(start, stop):
            body(step)
    else:
        lax.fori_loop(start, stop, lambda step, carry: (body(step), carry)[1], 0)


def kernel(
    tiles,
    chans,
    width,
    pts_ref,
    dest_ref,
    voxel_ref,
    weight_ref,
    grad_ref,
    out_ref,
    wgrad_ref,
    codes,
    pts_all,
    sums,
    grid,
    shifts,
    moved,
    taps,
    masked,
    partial,
    total,
    sending,
    received,
    pts_send,
    pts_recv,
    code_send,
    code_recv,
    grid_send,
    grid_recv,
    grad_send,
    grad_recv,
):
    me = lax.axis_index("tile")
    mine = lax.axis_index("chan")
    part = pts_ref.shape[0]
    outs = grad_ref.shape[0]
    channels = part * chans
    span = sending.shape[2]

    def peer(step):
        return lax.rem(me + step, tiles)

    def giver(step):
        return lax.rem(me + tiles - step, tiles)

    def chan_peer(step):
        return lax.rem(mine + step, chans)

    barrier = pltpu.get_barrier_semaphore()

    def greet(step):
        pl.semaphore_signal(barrier, inc=1, device_id={"tile": peer(step)})

    def greet_chan(step):
        pl.semaphore_signal(barrier, inc=1, device_id={"chan": chan_peer(step)})

    repeat(1, tiles, greet)
    repeat(1, chans, greet_chan)
    codes[me] = dest_ref[...] * VOX + voxel_ref[...]
    pl.semaphore_wait(barrier, tiles + chans - 2)

    def code_copy(step):
        return pltpu.make_async_remote_copy(
            src_ref=codes.at[me],
            dst_ref=codes.at[me],
            send_sem=code_send.at[step],
            recv_sem=code_recv.at[step],
            device_id={"tile": peer(step)},
        )

    def pts_copy(step):
        return pltpu.make_async_remote_copy(
            src_ref=pts_ref,
            dst_ref=pts_all.at[me],
            send_sem=pts_send.at[step],
            recv_sem=pts_recv.at[step],
            device_id={"tile": peer(step)},
        )

    def send_points(step):
        code_copy(step).start()
        pts_copy(step).start()

    repeat(1, tiles, send_points)

    for a in range(3):
        for tap in range(9):
            taps[a * outs : (a + 1) * outs, tap * channels : (tap + 1) * channels] = weight_ref[
                9 * a + tap
            ]
    to = lax.broadcasted_iota(jnp.int32, (PLANE, PLANE), 0)
    source = lax.broadcasted_iota(jnp.int32, (PLANE, PLANE), 1)
    for e in (-1, 0, 1):
        line = (to & (EDGE - 1)) + e
        here = (source == to + e) & (line >= 0) & (line < EDGE)
        shifts[(e + 1) * PLANE : (e + 2) * PLANE, :] = here.astype(jnp.float32).astype(jnp.bfloat16)
    edge = jnp.zeros((EDGE, moved.shape[2]), jnp.bfloat16)
    for plane in range(DEPTH):
        moved[plane, :EDGE, :] = edge
        moved[plane, PADDED - EDGE :, :] = edge
    masked[0] = jnp.zeros((outs, PLANE), jnp.bfloat16)
    masked[DEPTH + 1] = jnp.zeros((outs, PLANE), jnp.bfloat16)

    def add_points(features, code):
        rel = code - me * VOX
        high = rel >> 8
        low = rel & (PLANE - 1)
        count = features.shape[1]
        wide = features.astype(jnp.float32)
        rows = [jnp.where(high == h, wide, 0.0).astype(jnp.bfloat16) for h in range(DEPTH)]
        rank = lax.broadcasted_iota(jnp.int32, (2 * DEPTH, count), 0)
        rows.append((rank == high).astype(jnp.float32).astype(jnp.bfloat16))
        cell = lax.broadcasted_iota(jnp.int32, (PLANE, count), 0)
        onehot = (cell == low).astype(jnp.float32).astype(jnp.bfloat16)
        return lax.dot_general(
            jnp.concatenate(rows, axis=0), onehot, ROWS_MAJOR, preferred_element_type=jnp.float32
        )

    sums[...] = add_points(pts_ref[...], codes[me])

    def take_points(step):
        code_copy(step).wait_recv()
        pts_copy(step).wait_recv()
        origin = giver(step)
        sums[...] += add_points(pts_all[origin], codes[origin])

    repeat(1, tiles, take_points)

    counts = sums[DEPTH * part : DEPTH * part + DEPTH, :]
    floor = jnp.maximum(counts, 1.0)
    occupied = (counts > 0).astype(jnp.float32)
    held = grid.shape[2]

    def grid_copy(chunk, step):
        planes = pl.ds(chunk * PER_CHUNK, PER_CHUNK)
        return pltpu.make_async_remote_copy(
            src_ref=grid.at[planes, mine],
            dst_ref=grid.at[planes, mine],
            send_sem=grid_send.at[chunk, step],
            recv_sem=grid_recv.at[chunk, step],
            device_id={"chan": chan_peer(step)},
        )

    for chunk in range(CHUNKS):
        for plane in range(chunk * PER_CHUNK, (chunk + 1) * PER_CHUNK):
            mean = sums[plane * part : (plane + 1) * part, :] / floor[plane : plane + 1, :]
            if held > part:
                mean = jnp.concatenate([mean, jnp.zeros((held - part, PLANE), jnp.float32)], axis=0)
            grid[plane, mine] = mean.astype(jnp.bfloat16)
        for step in range(1, chans):
            grid_copy(chunk, step).start()

    for plane in range(DEPTH):
        kept = grad_ref[:, plane * PLANE : (plane + 1) * PLANE].astype(jnp.float32)
        masked[plane + 1] = (kept * occupied[plane : plane + 1, :]).astype(jnp.bfloat16)

    for chunk in range(CHUNKS):
        for step in range(1, chans):
            grid_copy(chunk, step).wait_recv()
        for plane in range(chunk * PER_CHUNK, (chunk + 1) * PER_CHUNK):
            if held > part:
                lanes = [grid[plane, c].astype(jnp.float32)[:part] for c in range(chans)]
                voxels = jnp.concatenate(lanes, axis=0).astype(jnp.bfloat16)
            else:
                voxels = grid[plane].reshape(channels, PLANE)
            lines = lax.dot_general(
                shifts[...], voxels, ROWS_MAJOR, preferred_element_type=jnp.float32
            ).astype(jnp.bfloat16)
            for e in range(3):
                moved[plane, EDGE : EDGE + PLANE, e * channels : (e + 1) * channels] = lines[
                    e * PLANE : (e + 1) * PLANE, :
                ]
            columns = jnp.concatenate(
                [moved[plane, b * EDGE : b * EDGE + PLANE, :] for b in range(3)], axis=1
            )
            partial[plane] = lax.dot_general(
                taps[...], columns, ROWS_MAJOR, preferred_element_type=jnp.float32
            )
            cotangents = jnp.concatenate([masked[plane + 2], masked[plane + 1], masked[plane]], axis=0)
            grads = jnp.dot(cotangents, columns, preferred_element_type=jnp.float32)
            for a in range(3):
                place = slice(a * 9 * channels, (a + 1) * 9 * channels)
                piece = grads[a * outs : (a + 1) * outs, :]
                if plane == 0:
                    total[:, place] = piece
                else:
                    total[:, place] += piece
    total[:, 27 * channels :] = jnp.zeros((outs, total.shape[1] - 27 * channels), jnp.float32)

    def block(owner):
        first = owner * width
        base = pl.multiple_of(first // 128 * 128, 128)
        window = total[:, pl.ds(base, span + 128)]
        return pltpu.roll(window, span + 128 - lax.rem(first, 128), 1)[:, :span]

    def grad_copy(step):
        return pltpu.make_async_remote_copy(
            src_ref=sending.at[step],
            dst_ref=received.at[step],
            send_sem=grad_send.at[step],
            recv_sem=grad_recv.at[step],
            device_id={"tile": peer(step)},
        )

    def send_grads(step):
        sending[step] = block(peer(step)).astype(jnp.bfloat16)
        grad_copy(step).start()

    repeat(1, tiles, send_grads)

    for plane in range(DEPTH):
        output = partial[plane, outs : 2 * outs, :]
        if plane > 0:
            output = output + partial[plane - 1, :outs, :]
        if plane < DEPTH - 1:
            output = output + partial[plane + 1, 2 * outs :, :]
        out_ref[:, plane * PLANE : (plane + 1) * PLANE] = (
            output * occupied[plane : plane + 1, :]
        ).astype(jnp.bfloat16)

    total[:, :span] = block(me)

    def take_grads(step):
        grad_copy(step).wait_recv()
        total[:, :span] += received[step].astype(jnp.float32)

    repeat(1, tiles, take_grads)
    wgrad_ref[...] = total[:, :width]

    def sent(step):
        code_copy(step).wait_send()
        pts_copy(step).wait_send()
        grad_copy(step).wait_send()

    repeat(1, tiles, sent)
    for chunk in range(CHUNKS):
        for step in range(1, chans):
            grid_copy(chunk, step).wait_send()


def on_device(points, dest, voxel, weight, grad_out):
    tiles, chans = lax.axis_size("tile"), lax.axis_size("chan")
    part, count = points.shape
    outs = grad_out.shape[0]
    channels = part * chans
    width = 27 * channels // tiles
    span = -(-width // 128) * 128
    total_width = max(((tiles - 1) * width // 128) * 128 + span + 128, 27 * channels + 128)
    vmem = pl.BlockSpec(memory_space=pltpu.VMEM)
    dma = pltpu.SemaphoreType.DMA
    return pl.pallas_call(
        functools.partial(kernel, tiles, chans, width),
        out_shape=(
            jax.ShapeDtypeStruct((outs, VOX), jnp.bfloat16),
            jax.ShapeDtypeStruct((outs, width), jnp.float32),
        ),
        in_specs=[vmem] * 5,
        out_specs=(vmem, vmem),
        scratch_shapes=[
            pltpu.VMEM((tiles, 1, count), jnp.int32),
            pltpu.VMEM((tiles, part, count), jnp.bfloat16),
            pltpu.VMEM((DEPTH * part + 2 * DEPTH, PLANE), jnp.float32),
            pltpu.VMEM((DEPTH, chans, max(part, 16), PLANE), jnp.bfloat16),
            pltpu.VMEM((3 * PLANE, PLANE), jnp.bfloat16),
            pltpu.VMEM((DEPTH, PADDED, 3 * channels), jnp.bfloat16),
            pltpu.VMEM((3 * outs, 9 * channels), jnp.bfloat16),
            pltpu.VMEM((DEPTH + 2, outs, PLANE), jnp.bfloat16),
            pltpu.VMEM((DEPTH, 3 * outs, PLANE), jnp.float32),
            pltpu.VMEM((outs, total_width), jnp.float32),
            pltpu.VMEM((tiles, outs, span), jnp.bfloat16),
            pltpu.VMEM((tiles, outs, span), jnp.bfloat16),
            dma((tiles,)),
            dma((tiles,)),
            dma((tiles,)),
            dma((tiles,)),
            dma((CHUNKS, chans)),
            dma((CHUNKS, chans)),
            dma((tiles,)),
            dma((tiles,)),
        ],
        compiler_params=pltpu.CompilerParams(
            collective_id=0, has_side_effects=True, vmem_limit_bytes=40 * 1024 * 1024
        ),
    )(
        points,
        dest.reshape(1, count),
        voxel.reshape(1, count),
        jnp.transpose(weight, (1, 0, 2)),
        grad_out,
    )


def solution(mesh):
    placed = (
        P("chan", "tile"),
        P("tile", None),
        P("tile", None),
        P("chan", None, None),
        P("chan", "tile"),
    )
    return jax.shard_map(
        on_device,
        mesh=mesh,
        in_specs=placed,
        out_specs=(P("chan", "tile"), P("chan", "tile")),
        check_vma=False,
    )
```

time: 216 us -> 42.7 us (0.20)
  local copies, waits for them, and re-layouts: 89.2 us -> 5.53 us
  other arithmetic: 40.1 us -> 0 us
  Pallas kernels: 0 us -> 36.3 us
  waiting for transfers between devices: 33.8 us -> 0 us
  between operations: 14.5 us -> 0.65 us
  blocking collectives: 12.4 us -> 0 us
  matrix products: 12.3 us -> 0 us
  starting transfers between devices: 11.2 us -> 0 us
    another operation x27 -> x0, local copies, waits for them, and re-layouts: 50.5 us -> none  [tile_conv(): jnp.stack(stacked, axis=0).reshape(27 * count, DEPTH * EDGE * EDGE)]
    pallas_call x0 -> x1, Pallas kernels: none -> 36.3 us  [on_device(): pl.pallas_call(functools.partial(kernel, tiles, chans, width), out_shape=...]
    scatter-add x2 -> x0, other arithmetic: 33.8 us -> none  [the longest x1 17.2 us: voxelize(): sums = jnp.zeros((features.shape[0], VOX), jnp.float32).at[:, cells].add(...]
    unnamed x2 -> x0, waiting for transfers between devices: 33.8 us -> none
    unnamed x61 -> x12, local copies, waits for them, and re-layouts: 27.1 us -> 5.53 us
    all_gather x1 -> x0, blocking collectives: 12.4 us -> none  [on_device(): all_channels = lax.all_gather(points, 'chan', axis=0, tiled=True)]
    all_to_all x2 -> x0, starting transfers between devices: 11.2 us -> none  [the longest x1 6 us: on_device(): lax.all_to_all(send, 'tile', split_axis=1, concat_axis=1, tiled=True)]
    dot_general x1 -> x0, matrix products: 7.15 us -> none  [tile_conv(): jnp.dot(weight_part.reshape(out_rows, 27 * count), columns, preferred_ele...]
  transfers between devices with their start and end apart: 3 -> 0, of which waited for: 1 -> 0; matrix products, arithmetic and copies ran while one was open for 13% -> 0% of each run, Pallas kernels for 0% -> 0%
where the time goes in v1:
time: 42.7 us; the launch traced here: 42.4 us
  Pallas kernels  36.3 us (85%)
  local copies, waits for them, and re-layouts  5.53 us (13%)
  between operations  0.65 us (2%)
    pallas_call x1, Pallas kernels, on_device(): pl.pallas_call(functools.partial(kernel, tiles, chans, width), out_shape=...  36.3 us
    unnamed x12, local copies, waits for them, and re-layouts  5.53 us

profile of v1, /device:TPU:1, one launch (start us, length us, event | category | flops | bytes accessed | tf_op | source)
XLA Modules:
  0.0 42.4 jit_solution(2632555644657563361)
XLA Ops:
  0.6 0.0 copy-start.3
  0.6 0.7 %copy-done.3 = s32[1024,1]{0,1:T(1,128)S(1)} copy-done((s32[1024,1]{0,1:T(1,128)S(1)}, s32[1024,1]{0,1:T(1,128)}, u32[]{:S(2)}) %copy-start.3) | copy-done | bytes 4120
  1.3 0.0 copy-start
  1.3 1.0 %copy-done = bf16[64,27,128]{2,0,1:T(8,128)(2,1)S(1)} copy-done((bf16[64,27,128]{2,0,1:T(8,128)(2,1)S(1)}, bf16[64,27,128]{2,0,1:T(8,128)(2,1)}, u32[]{:S(2)}) %copy-start) | copy-done | bytes 442392
  2.3 0.0 copy-start.1
  2.3 0.9 %copy-done.1 = bf16[64,2048]{1,0:T(8,128)(2,1)S(1)} copy-done((bf16[64,2048]{1,0:T(8,128)(2,1)S(1)}, bf16[64,2048]{1,0:T(8,128)(2,1)}, u32[]{:S(2)}) %copy-start.1) | copy-done | bytes 262168
  3.3 0.0 copy-start.2
  3.3 0.8 %copy-done.2 = bf16[32,1024]{1,0:T(8,128)(2,1)S(1)} copy-done((bf16[32,1024]{1,0:T(8,128)(2,1)S(1)}, bf16[32,1024]{1,0:T(8,128)(2,1)}, u32[]{:S(2)}) %copy-start.2) | copy-done | bytes 65560
  4.1 0.0 copy-start.4
  4.1 0.7 %copy-done.4 = s32[1024,1]{0,1:T(1,128)S(1)} copy-done((s32[1024,1]{0,1:T(1,128)S(1)}, s32[1024,1]{0,1:T(1,128)}, u32[]{:S(2)}) %copy-start.4) | copy-done | bytes 4120
  4.8 36.3 %shard_map.68 = (bf16[64,2048]{1,0:T(8,128)(2,1)S(1)}, f32[64,432]{1,0:T(8,128)S(1)}) custom-call(bf16[32,1024]{1,0:T(8,128)(2,1)S(1)} %copy-done.2, s32[1,1024]{1,0:T(1,128)S(1)} %bitcast.4, s32[1,1024]{1,0:T(1,128)S(1)} %bitcast.5, bf16[27,64,128]{2,1,0:T(8,128)(2,1)S(1)} %bitcast.3, bf16[64,2048]{1,0:T(8,128)(2,1)S(1)} %copy-done.1), custom_call_target="tpu_custom_call" | custom-call | tf_op jit(solution)/shard_map/pallas_call | solution.py:278
  41.1 0.7 %copy.9 = bf16[64,2048]{1,0:T(8,128)(2,1)} copy(bf16[64,2048]{1,0:T(8,128)(2,1)S(1)} %get-tuple-element.4) | data formatting | bytes 524288
  41.8 0.7 %copy.10 = f32[64,432]{1,0:T(8,128)} copy(f32[64,432]{1,0:T(8,128)S(1)} %get-tuple-element.5) | data formatting | bytes 221184
Async XLA Ops:
  0.6 0.7 %copy-start.3 = (s32[1024,1]{0,1:T(1,128)S(1)}, s32[1024,1]{0,1:T(1,128)}, u32[]{:S(2)}) copy-start(s32[1024,1]{0,1:T(1,128)} %param.6) | copy-start | bytes 12292
  1.3 1.0 %copy-start = (bf16[64,27,128]{2,0,1:T(8,128)(2,1)S(1)}, bf16[64,27,128]{2,0,1:T(8,128)(2,1)}, u32[]{:S(2)}) copy-start(bf16[64,27,128]{2,0,1:T(8,128)(2,1)} %param.8) | copy-start | bytes 1327108
  2.3 0.9 %copy-start.1 = (bf16[64,2048]{1,0:T(8,128)(2,1)S(1)}, bf16[64,2048]{1,0:T(8,128)(2,1)}, u32[]{:S(2)}) copy-start(bf16[64,2048]{1,0:T(8,128)(2,1)} %grad_ref.1) | copy-start | bytes 786436
  3.3 0.8 %copy-start.2 = (bf16[32,1024]{1,0:T(8,128)(2,1)S(1)}, bf16[32,1024]{1,0:T(8,128)(2,1)}, u32[]{:S(2)}) copy-start(bf16[32,1024]{1,0:T(8,128)(2,1)} %pts_ref.1) | copy-start | bytes 196612
  4.1 0.7 %copy-start.4 = (s32[1024,1]{0,1:T(1,128)S(1)}, s32[1024,1]{0,1:T(1,128)}, u32[]{:S(2)}) copy-start(s32[1024,1]{0,1:T(1,128)} %param.7) | copy-start | bytes 12292

commit v2 on v1

--- a/solution.py
+++ b/solution.py
@@ -36,6 +36,10 @@
     grad_ref,
     out_ref,
     wgrad_ref,
+    dest_here,
+    voxel_here,
+    weight_here,
+    grad_here,
     codes,
     pts_all,
     sums,
@@ -46,14 +50,21 @@
     masked,
     partial,
     total,
+    handing,
+    handed,
     sending,
     received,
+    local_sem,
     pts_send,
     pts_recv,
+    share_send,
+    share_recv,
     code_send,
     code_recv,
     grid_send,
     grid_recv,
+    hand_send,
+    hand_recv,
     grad_send,
     grad_recv,
 ):
@@ -63,6 +74,9 @@
     outs = grad_ref.shape[0]
     channels = part * chans
     span = sending.shape[2]
+    chips = tiles // 2
+    chip, core = me // 2, lax.rem(me, 2)
+    sibling = 2 * chip + 1 - core
 
     def peer(step):
         return lax.rem(me + step, tiles)
@@ -70,6 +84,12 @@
     def giver(step):
         return lax.rem(me + tiles - step, tiles)
 
+    def chip_peer(step):
+        return lax.rem(chip + step, chips)
+
+    def chip_giver(step):
+        return lax.rem(chip + chips - step, chips)
+
     def chan_peer(step):
         return lax.rem(mine + step, chans)
 
@@ -81,9 +101,23 @@
     def greet_chan(step):
         pl.semaphore_signal(barrier, inc=1, device_id={"chan": chan_peer(step)})
 
+    def local(place, source, target):
+        return pltpu.make_async_copy(source, target, local_sem.at[place])
+
+    fetched = [
+        local(0, dest_ref, dest_here),
+        local(1, voxel_ref, voxel_here),
+        local(2, pts_ref, pts_all.at[me]),
+        local(3, weight_ref, weight_here),
+        local(4, grad_ref, grad_here),
+    ]
+    for copy in fetched:
+        copy.start()
     repeat(1, tiles, greet)
     repeat(1, chans, greet_chan)
-    codes[me] = dest_ref[...] * VOX + voxel_ref[...]
+    fetched[0].wait()
+    fetched[1].wait()
+    codes[me] = dest_here[...] * VOX + voxel_here[...]
     pl.semaphore_wait(barrier, tiles + chans - 2)
 
     def code_copy(step):
@@ -101,18 +135,28 @@
             dst_ref=pts_all.at[me],
             send_sem=pts_send.at[step],
             recv_sem=pts_recv.at[step],
-            device_id={"tile": peer(step)},
-        )
-
-    def send_points(step):
-        code_copy(step).start()
-        pts_copy(step).start()
-
-    repeat(1, tiles, send_points)
+            device_id={"tile": 2 * chip_peer(step) + core},
+        )
+
+    def share_copy(step):
+        origin = 2 * chip_giver(step) + core
+        return pltpu.make_async_remote_copy(
+            src_ref=pts_all.at[origin],
+            dst_ref=pts_all.at[origin],
+            send_sem=share_send.at[step],
+            recv_sem=share_recv.at[step],
+            device_id={"tile": sibling},
+        )
+
+    repeat(1, chips, lambda step: pts_copy(step).start())
+    repeat(1, tiles, lambda step: code_copy(step).start())
+    fetched[2].wait()
+    share_copy(0).start()
+    fetched[3].wait()
 
     for a in range(3):
         for tap in range(9):
-            taps[a * outs : (a + 1) * outs, tap * channels : (tap + 1) * channels] = weight_ref[
+            taps[a * outs : (a + 1) * outs, tap * channels : (tap + 1) * channels] = weight_here[
                 9 * a + tap
             ]
     to = lax.broadcasted_iota(jnp.int32, (PLANE, PLANE), 0)
@@ -143,15 +187,24 @@
             jnp.concatenate(rows, axis=0), onehot, ROWS_MAJOR, preferred_element_type=jnp.float32
         )
 
-    sums[...] = add_points(pts_ref[...], codes[me])
-
-    def take_points(step):
-        code_copy(step).wait_recv()
+    sums[...] = add_points(pts_all[me], codes[me])
+    repeat(1, tiles, lambda step: code_copy(step).wait_recv())
+
+    def take_points(origin):
+        sums[...] += add_points(pts_all[origin], codes[origin])
+
+    def take_shared(step):
+        share_copy(step).wait_recv()
+        take_points(2 * chip_giver(step) + 1 - core)
+
+    def take_sent(step):
         pts_copy(step).wait_recv()
-        origin = giver(step)
-        sums[...] += add_points(pts_all[origin], codes[origin])
-
-    repeat(1, tiles, take_points)
+        share_copy(step).start()
+        take_points(2 * chip_giver(step) + core)
+
+    take_shared(0)
+    repeat(1, chips, take_sent)
+    repeat(1, chips, take_shared)
 
     counts = sums[DEPTH * part : DEPTH * part + DEPTH, :]
     floor = jnp.maximum(counts, 1.0)
@@ -177,8 +230,9 @@
         for step in range(1, chans):
             grid_copy(chunk, step).start()
 
+    fetched[4].wait()
     for plane in range(DEPTH):
-        kept = grad_ref[:, plane * PLANE : (plane + 1) * PLANE].astype(jnp.float32)
+        kept = grad_here[:, plane * PLANE : (plane + 1) * PLANE].astype(jnp.float32)
         masked[plane + 1] = (kept * occupied[plane : plane + 1, :]).astype(jnp.bfloat16)
 
     for chunk in range(CHUNKS):
@@ -220,20 +274,37 @@
         window = total[:, pl.ds(base, span + 128)]
         return pltpu.roll(window, span + 128 - lax.rem(first, 128), 1)[:, :span]
 
+    def hand_copy(step):
+        return pltpu.make_async_remote_copy(
+            src_ref=handing.at[step],
+            dst_ref=handed.at[step],
+            send_sem=hand_send.at[step],
+            recv_sem=hand_recv.at[step],
+            device_id={"tile": sibling},
+        )
+
     def grad_copy(step):
         return pltpu.make_async_remote_copy(
             src_ref=sending.at[step],
             dst_ref=received.at[step],
             send_sem=grad_send.at[step],
             recv_sem=grad_recv.at[step],
-            device_id={"tile": peer(step)},
-        )
+            device_id={"tile": 2 * chip_peer(step) + core},
+        )
+
+    def hand_grads(step):
+        handing[step] = block(2 * chip_peer(step) + 1 - core)
+        hand_copy(step).start()
 
     def send_grads(step):
-        sending[step] = block(peer(step)).astype(jnp.bfloat16)
+        own = block(2 * chip_peer(step) + core)
+        hand_copy(step).wait_recv()
+        sending[step] = (own + handed[step]).astype(jnp.bfloat16)
         grad_copy(step).start()
 
-    repeat(1, tiles, send_grads)
+    repeat(1, chips, hand_grads)
+    hand_grads(0)
+    repeat(1, chips, send_grads)
 
     for plane in range(DEPTH):
         output = partial[plane, outs : 2 * outs, :]
@@ -245,21 +316,28 @@
             output * occupied[plane : plane + 1, :]
         ).astype(jnp.bfloat16)
 
-    total[:, :span] = block(me)
+    own_block = block(me)
+    hand_copy(0).wait_recv()
+    total[:, :span] = own_block + handed[0]
 
     def take_grads(step):
         grad_copy(step).wait_recv()
         total[:, :span] += received[step].astype(jnp.float32)
 
-    repeat(1, tiles, take_grads)
+    repeat(1, chips, take_grads)
     wgrad_ref[...] = total[:, :width]
 
     def sent(step):
-        code_copy(step).wait_send()
         pts_copy(step).wait_send()
         grad_copy(step).wait_send()
 
-    repeat(1, tiles, sent)
+    def handed_over(step):
+        share_copy(step).wait_send()
+        hand_copy(step).wait_send()
+
+    repeat(1, tiles, lambda step: code_copy(step).wait_send())
+    repeat(1, chips, sent)
+    repeat(0, chips, handed_over)
     for chunk in range(CHUNKS):
         for step in range(1, chans):
             grid_copy(chunk, step).wait_send()
@@ -273,6 +351,8 @@
     width = 27 * channels // tiles
     span = -(-width // 128) * 128
     total_width = max(((tiles - 1) * width // 128) * 128 + span + 128, 27 * channels + 128)
+    chips = tiles // 2
+    hbm = pl.BlockSpec(memory_space=pltpu.HBM)
     vmem = pl.BlockSpec(memory_space=pltpu.VMEM)
     dma = pltpu.SemaphoreType.DMA
     return pl.pallas_call(
@@ -281,9 +361,13 @@
             jax.ShapeDtypeStruct((outs, VOX), jnp.bfloat16),
             jax.ShapeDtypeStruct((outs, width), jnp.float32),
         ),
-        in_specs=[vmem] * 5,
+        in_specs=[hbm] * 5,
         out_specs=(vmem, vmem),
         scratch_shapes=[
+            pltpu.VMEM((1, count), jnp.int32),
+            pltpu.VMEM((1, count), jnp.int32),
+            pltpu.VMEM((27, outs, channels), jnp.bfloat16),
+            pltpu.VMEM((outs, VOX), jnp.bfloat16),
             pltpu.VMEM((tiles, 1, count), jnp.int32),
             pltpu.VMEM((tiles, part, count), jnp.bfloat16),
             pltpu.VMEM((DEPTH * part + 2 * DEPTH, PLANE), jnp.float32),
@@ -294,19 +378,26 @@
             pltpu.VMEM((DEPTH + 2, outs, PLANE), jnp.bfloat16),
             pltpu.VMEM((DEPTH, 3 * outs, PLANE), jnp.float32),
             pltpu.VMEM((outs, total_width), jnp.float32),
-            pltpu.VMEM((tiles, outs, span), jnp.bfloat16),
-            pltpu.VMEM((tiles, outs, span), jnp.bfloat16),
-            dma((tiles,)),
-            dma((tiles,)),
+            pltpu.VMEM((chips, outs, span), jnp.float32),
+            pltpu.VMEM((chips, outs, span), jnp.float32),
+            pltpu.VMEM((chips, outs, span), jnp.bfloat16),
+            pltpu.VMEM((chips, outs, span), jnp.bfloat16),
+            dma((5,)),
+            dma((chips,)),
+            dma((chips,)),
+            dma((chips,)),
+            dma((chips,)),
             dma((tiles,)),
             dma((tiles,)),
             dma((CHUNKS, chans)),
             dma((CHUNKS, chans)),
-            dma((tiles,)),
-            dma((tiles,)),
+            dma((chips,)),
+            dma((chips,)),
+            dma((chips,)),
+            dma((chips,)),
         ],
         compiler_params=pltpu.CompilerParams(
-            collective_id=0, has_side_effects=True, vmem_limit_bytes=40 * 1024 * 1024
+            collective_id=0, has_side_effects=True, vmem_limit_bytes=64 * 1024 * 1024
         ),
     )(
         points,

time: 42.7 us -> 38.7 us (0.906)
  local copies, waits for them, and re-layouts: 5.53 us -> 2.36 us
  Pallas kernels: 36.3 us -> 35.2 us
    unnamed x12 -> x4, local copies, waits for them, and re-layouts: 5.53 us -> 2.36 us
    pallas_call x1, Pallas kernels: 36.3 us -> 35.2 us  [on_device(): pl.pallas_call(functools.partial(kernel, tiles, chans, width), out_shape=...]
where the time goes in v2:
time: 38.7 us; the launch traced here: 38.2 us
  Pallas kernels  35.2 us (91%)
  local copies, waits for them, and re-layouts  2.36 us (6%)
  between operations  0.65 us (2%)
    pallas_call x1, Pallas kernels, on_device(): pl.pallas_call(functools.partial(kernel, tiles, chans, width), out_shape=...  35.2 us
    unnamed x4, local copies, waits for them, and re-layouts  2.36 us

profile of v2, /device:TPU:1, one launch (start us, length us, event | category | flops | bytes accessed | tf_op | source)
XLA Modules:
  0.0 38.2 jit_solution(17058564478134674058)
XLA Ops:
  0.6 35.2 %shard_map.68 = (bf16[64,2048]{1,0:T(8,128)(2,1)}, f32[64,432]{1,0:T(8,128)}) custom-call(bf16[32,1024]{1,0:T(8,128)(2,1)} %pts_ref.1, s32[1,1024]{1,0:T(1,128)} %bitcast.4, s32[1,1024]{1,0:T(1,128)} %bitcast.5, bf16[27,64,128]{2,1,0:T(8,128)(2,1)} %bitcast.3, bf16[64,2048]{1,0:T(8,128)(2,1)} %grad_ref.1), custom_call_target="tpu_custom_call" | custom-call | tf_op jit(solution)/shard_map/pallas_call | solution.py:358
  35.8 0.0 copy-start
  35.9 1.7 %copy.9 = bf16[64,2048]{1,0:T(8,128)(2,1)} copy(bf16[64,2048]{1,0:T(8,128)(2,1)} %get-tuple-element.4) | data formatting | bytes 524288
  37.6 0.0 copy-done
  37.6 0.7 %copy.10 = f32[64,432]{1,0:T(8,128)} copy(f32[64,432]{1,0:T(8,128)S(1)} %copy-done) | data formatting | bytes 221184
Async XLA Ops:
  35.8 1.7 %copy-start = (f32[64,432]{1,0:T(8,128)S(1)}, f32[64,432]{1,0:T(8,128)}, u32[]{:S(2)}) copy-start(f32[64,432]{1,0:T(8,128)} %get-tuple-element.5) | copy-start | bytes 331780

commit v3 on v2

--- a/solution.py
+++ b/solution.py
@@ -12,7 +12,8 @@
 PLANE = EDGE * EDGE
 VOX = DEPTH * PLANE
 PADDED = PLANE + 2 * EDGE
-CHUNKS = 4
+CHUNKS = 8
+LATE = 4
 PER_CHUNK = DEPTH // CHUNKS
 ROWS_MAJOR = (((1,), (1,)), ((), ()))
 
@@ -63,6 +64,7 @@
     code_recv,
     grid_send,
     grid_recv,
+    relay_send,
     hand_send,
     hand_recv,
     grad_send,
@@ -221,22 +223,65 @@
             device_id={"chan": chan_peer(step)},
         )
 
+    chain = chans == 4
+    inner = (mine == 1) | (mine == 2)
+
+    def direct(step, act):
+        if chain and step == 1:
+            pl.when(mine != 3)(act)
+        elif chain and step == 3:
+            pl.when(mine != 0)(act)
+        else:
+            act()
+
+    def relay_copy(chunk):
+        planes = pl.ds(chunk * PER_CHUNK, PER_CHUNK)
+        origin = lax.rem(mine + 2, chans)
+        return pltpu.make_async_remote_copy(
+            src_ref=grid.at[planes, origin],
+            dst_ref=grid.at[planes, origin],
+            send_sem=relay_send.at[chunk],
+            recv_sem=grid_recv.at[chunk, jnp.where(mine == 1, 1, 3)],
+            device_id={"chan": jnp.where(mine == 1, 0, 3)},
+        )
+
+    def pass_on(chunk):
+        grid_copy(chunk, 2).wait_recv()
+
+        @pl.when(inner)
+        def _():
+            relay_copy(chunk).start()
+
     for chunk in range(CHUNKS):
         for plane in range(chunk * PER_CHUNK, (chunk + 1) * PER_CHUNK):
             mean = sums[plane * part : (plane + 1) * part, :] / floor[plane : plane + 1, :]
             if held > part:
                 mean = jnp.concatenate([mean, jnp.zeros((held - part, PLANE), jnp.float32)], axis=0)
             grid[plane, mine] = mean.astype(jnp.bfloat16)
-        for step in range(1, chans):
-            grid_copy(chunk, step).start()
+        for step in (2, 1, 3) if chain else range(1, chans):
+            direct(step, grid_copy(chunk, step).start)
 
     fetched[4].wait()
     for plane in range(DEPTH):
         kept = grad_here[:, plane * PLANE : (plane + 1) * PLANE].astype(jnp.float32)
         masked[plane + 1] = (kept * occupied[plane : plane + 1, :]).astype(jnp.bfloat16)
 
+    def columns_of(plane):
+        return jnp.concatenate(
+            [moved[plane, b * EDGE : b * EDGE + PLANE, :] for b in range(3)], axis=1
+        )
+
+    def forward(plane, columns):
+        partial[plane] = lax.dot_general(
+            taps[...], columns, ROWS_MAJOR, preferred_element_type=jnp.float32
+        )
+
+    if chain:
+        pass_on(0)
     for chunk in range(CHUNKS):
-        for step in range(1, chans):
+        if chain and chunk + 1 < CHUNKS:
+            pass_on(chunk + 1)
+        for step in (1, 3) if chain else range(1, chans):
             grid_copy(chunk, step).wait_recv()
         for plane in range(chunk * PER_CHUNK, (chunk + 1) * PER_CHUNK):
             if held > part:
@@ -251,12 +296,9 @@
                 moved[plane, EDGE : EDGE + PLANE, e * channels : (e + 1) * channels] = lines[
                     e * PLANE : (e + 1) * PLANE, :
                 ]
-            columns = jnp.concatenate(
-                [moved[plane, b * EDGE : b * EDGE + PLANE, :] for b in range(3)], axis=1
-            )
-            partial[plane] = lax.dot_general(
-                taps[...], columns, ROWS_MAJOR, preferred_element_type=jnp.float32
-            )
+            columns = columns_of(plane)
+            if plane < DEPTH - LATE:
+                forward(plane, columns)
             cotangents = jnp.concatenate([masked[plane + 2], masked[plane + 1], masked[plane]], axis=0)
             grads = jnp.dot(cotangents, columns, preferred_element_type=jnp.float32)
             for a in range(3):
@@ -305,6 +347,8 @@
     repeat(1, chips, hand_grads)
     hand_grads(0)
     repeat(1, chips, send_grads)
+    for plane in range(DEPTH - LATE, DEPTH):
+        forward(plane, columns_of(plane))
 
     for plane in range(DEPTH):
         output = partial[plane, outs : 2 * outs, :]
@@ -340,7 +384,9 @@
     repeat(0, chips, handed_over)
     for chunk in range(CHUNKS):
         for step in range(1, chans):
-            grid_copy(chunk, step).wait_send()
+            direct(step, grid_copy(chunk, step).wait_send)
+        if chain:
+            pl.when(inner)(relay_copy(chunk).wait_send)
 
 
 def on_device(points, dest, voxel, weight, grad_out):
@@ -391,6 +437,7 @@
             dma((tiles,)),
             dma((CHUNKS, chans)),
             dma((CHUNKS, chans)),
+            dma((CHUNKS,)),
             dma((chips,)),
             dma((chips,)),
             dma((chips,)),

time: 38.7 us -> 37.6 us (0.972)
  Pallas kernels: 35.2 us -> 34 us
    pallas_call x1, Pallas kernels: 35.2 us -> 34 us  [on_device(): pl.pallas_call(functools.partial(kernel, tiles, chans, width), out_shape=...]
where the time goes in v3:
time: 37.6 us; the launch traced here: 37.1 us
  Pallas kernels  34 us (90%)
  local copies, waits for them, and re-layouts  2.36 us (6%)
  between operations  0.65 us (2%)
    pallas_call x1, Pallas kernels, on_device(): pl.pallas_call(functools.partial(kernel, tiles, chans, width), out_shape=...  34 us
    unnamed x4, local copies, waits for them, and re-layouts  2.36 us

profile of v3, /device:TPU:1, one launch (start us, length us, event | category | flops | bytes accessed | tf_op | source)
XLA Modules:
  0.0 37.1 jit_solution(7808145275031169319)
XLA Ops:
  0.6 34.0 %shard_map.68 = (bf16[64,2048]{1,0:T(8,128)(2,1)}, f32[64,432]{1,0:T(8,128)}) custom-call(bf16[32,1024]{1,0:T(8,128)(2,1)} %pts_ref.1, s32[1,1024]{1,0:T(1,128)} %bitcast.4, s32[1,1024]{1,0:T(1,128)} %bitcast.5, bf16[27,64,128]{2,1,0:T(8,128)(2,1)} %bitcast.3, bf16[64,2048]{1,0:T(8,128)(2,1)} %grad_ref.1), custom_call_target="tpu_custom_call" | custom-call | tf_op jit(solution)/shard_map/pallas_call | solution.py:404
  34.7 0.0 copy-start
  34.7 1.7 %copy.9 = bf16[64,2048]{1,0:T(8,128)(2,1)} copy(bf16[64,2048]{1,0:T(8,128)(2,1)} %get-tuple-element.4) | data formatting | bytes 524288
  36.4 0.0 copy-done
  36.4 0.7 %copy.10 = f32[64,432]{1,0:T(8,128)} copy(f32[64,432]{1,0:T(8,128)S(1)} %copy-done) | data formatting | bytes 221184
Async XLA Ops:
  34.7 1.7 %copy-start = (f32[64,432]{1,0:T(8,128)S(1)}, f32[64,432]{1,0:T(8,128)}, u32[]{:S(2)}) copy-start(f32[64,432]{1,0:T(8,128)} %get-tuple-element.5) | copy-start | bytes 331780

commit v4 on v3

--- a/solution.py
+++ b/solution.py
@@ -47,6 +47,7 @@
     grid,
     shifts,
     moved,
+    stacked,
     taps,
     masked,
     partial,
@@ -158,9 +159,12 @@
 
     for a in range(3):
         for tap in range(9):
-            taps[a * outs : (a + 1) * outs, tap * channels : (tap + 1) * channels] = weight_here[
+            stacked[a * outs : (a + 1) * outs, tap * channels : (tap + 1) * channels] = weight_here[
                 9 * a + tap
-            ]
+            ].astype(jnp.float32)
+    for tap in range(9):
+        place = slice(tap * channels, (tap + 1) * channels)
+        taps[place, :] = stacked[:, place].T.astype(jnp.bfloat16)
     to = lax.broadcasted_iota(jnp.int32, (PLANE, PLANE), 0)
     source = lax.broadcasted_iota(jnp.int32, (PLANE, PLANE), 1)
     for e in (-1, 0, 1):
@@ -272,9 +276,7 @@
         )
 
     def forward(plane, columns):
-        partial[plane] = lax.dot_general(
-            taps[...], columns, ROWS_MAJOR, preferred_element_type=jnp.float32
-        )
+        partial[plane] = jnp.dot(columns, taps[...], preferred_element_type=jnp.float32).T
 
     if chain:
         pass_on(0)
@@ -420,7 +422,8 @@
             pltpu.VMEM((DEPTH, chans, max(part, 16), PLANE), jnp.bfloat16),
             pltpu.VMEM((3 * PLANE, PLANE), jnp.bfloat16),
             pltpu.VMEM((DEPTH, PADDED, 3 * channels), jnp.bfloat16),
-            pltpu.VMEM((3 * outs, 9 * channels), jnp.bfloat16),
+            pltpu.VMEM((3 * outs, 9 * channels), jnp.float32),
+            pltpu.VMEM((9 * channels, 3 * outs), jnp.bfloat16),
             pltpu.VMEM((DEPTH + 2, outs, PLANE), jnp.bfloat16),
             pltpu.VMEM((DEPTH, 3 * outs, PLANE), jnp.float32),
             pltpu.VMEM((outs, total_width), jnp.float32),
@@ -444,14 +447,19 @@
             dma((chips,)),
         ],
         compiler_params=pltpu.CompilerParams(
-            collective_id=0, has_side_effects=True, vmem_limit_bytes=64 * 1024 * 1024
+            collective_id=0, has_side_effects=True, vmem_limit_bytes=48 * 1024 * 1024
         ),
     )(
-        points,
-        dest.reshape(1, count),
-        voxel.reshape(1, count),
-        jnp.transpose(weight, (1, 0, 2)),
-        grad_out,
+        *(
+            pltpu.with_memory_space_constraint(operand, pltpu.HBM)
+            for operand in (
+                points,
+                dest.reshape(1, count),
+                voxel.reshape(1, count),
+                jnp.transpose(weight, (1, 0, 2)),
+                grad_out,
+            )
+        )
     )
 
 

time: 37.6 us -> 35.9 us (0.955)
  local copies, waits for them, and re-layouts: 2.36 us -> 1.36 us
  Pallas kernels: 34 us -> 33.3 us
    unnamed x4 -> x2, local copies, waits for them, and re-layouts: 2.36 us -> 1.36 us
    pallas_call x1, Pallas kernels: 34 us -> 33.3 us  [on_device(): pl.pallas_call(functools.partial(kernel, tiles, chans, width), out_shape=...]
where the time goes in v4:
time: 35.9 us; the launch traced here: 35.3 us
  Pallas kernels  33.3 us (93%)
  local copies, waits for them, and re-layouts  1.36 us (4%)
  between operations  0.64 us (2%)
    pallas_call x1, Pallas kernels, on_device(): pl.pallas_call(functools.partial(kernel, tiles, chans, width), out_shape=...  33.3 us
    unnamed x2, local copies, waits for them, and re-layouts  1.36 us

profile of v4, /device:TPU:1, one launch (start us, length us, event | category | flops | bytes accessed | tf_op | source)
XLA Modules:
  0.0 35.3 jit_solution(11278944713999617370)
XLA Ops:
  0.6 33.3 %shard_map.68 = (bf16[64,2048]{1,0:T(8,128)(2,1)S(1)}, f32[64,432]{1,0:T(8,128)S(1)}) custom-call(bf16[32,1024]{1,0:T(8,128)(2,1)} %pts_ref.1, s32[1,1024]{1,0:T(1,128)} %bitcast.4, s32[1,1024]{1,0:T(1,128)} %bitcast.5, bf16[27,64,128]{2,1,0:T(8,128)(2,1)} %bitcast.3, bf16[64,2048]{1,0:T(8,128)(2,1)} %grad_ref.1), custom_call_target="tpu_custom_call" | custom-call | tf_op jit(solution)/shard_map/pallas_call | solution.py:406
  34.0 0.7 %copy.9 = bf16[64,2048]{1,0:T(8,128)(2,1)} copy(bf16[64,2048]{1,0:T(8,128)(2,1)S(1)} %get-tuple-element.4) | data formatting | bytes 524288
  34.7 0.7 %copy.10 = f32[64,432]{1,0:T(8,128)} copy(f32[64,432]{1,0:T(8,128)S(1)} %get-tuple-element.5) | data formatting | bytes 221184

commit v5 on v4

--- a/solution.py
+++ b/solution.py
@@ -13,7 +13,7 @@
 VOX = DEPTH * PLANE
 PADDED = PLANE + 2 * EDGE
 CHUNKS = 8
-LATE = 4
+LATE = 6
 PER_CHUNK = DEPTH // CHUNKS
 ROWS_MAJOR = (((1,), (1,)), ((), ()))
 
@@ -155,16 +155,7 @@
     repeat(1, tiles, lambda step: code_copy(step).start())
     fetched[2].wait()
     share_copy(0).start()
-    fetched[3].wait()
-
-    for a in range(3):
-        for tap in range(9):
-            stacked[a * outs : (a + 1) * outs, tap * channels : (tap + 1) * channels] = weight_here[
-                9 * a + tap
-            ].astype(jnp.float32)
-    for tap in range(9):
-        place = slice(tap * channels, (tap + 1) * channels)
-        taps[place, :] = stacked[:, place].T.astype(jnp.bfloat16)
+
     to = lax.broadcasted_iota(jnp.int32, (PLANE, PLANE), 0)
     source = lax.broadcasted_iota(jnp.int32, (PLANE, PLANE), 1)
     for e in (-1, 0, 1):
@@ -250,10 +241,9 @@
         )
 
     def pass_on(chunk):
-        grid_copy(chunk, 2).wait_recv()
-
         @pl.when(inner)
         def _():
+            grid_copy(chunk, 2).wait_recv()
             relay_copy(chunk).start()
 
     for chunk in range(CHUNKS):
@@ -265,6 +255,15 @@
         for step in (2, 1, 3) if chain else range(1, chans):
             direct(step, grid_copy(chunk, step).start)
 
+    fetched[3].wait()
+    for a in range(3):
+        for tap in range(9):
+            stacked[a * outs : (a + 1) * outs, tap * channels : (tap + 1) * channels] = weight_here[
+                9 * a + tap
+            ].astype(jnp.float32)
+    for tap in range(9):
+        place = slice(tap * channels, (tap + 1) * channels)
+        taps[place, :] = stacked[:, place].T.astype(jnp.bfloat16)
     fetched[4].wait()
     for plane in range(DEPTH):
         kept = grad_here[:, plane * PLANE : (plane + 1) * PLANE].astype(jnp.float32)
@@ -285,6 +284,8 @@
             pass_on(chunk + 1)
         for step in (1, 3) if chain else range(1, chans):
             grid_copy(chunk, step).wait_recv()
+        if chain:
+            pl.when(jnp.logical_not(inner))(grid_copy(chunk, 2).wait_recv)
         for plane in range(chunk * PER_CHUNK, (chunk + 1) * PER_CHUNK):
             if held > part:
                 lanes = [grid[plane, c].astype(jnp.float32)[:part] for c in range(chans)]

time: 35.9 us -> 35.9 us (level)
  no operation moved by 1% of the time
where the time goes in v5:
time: 35.9 us; the launch traced here: 35.4 us
  Pallas kernels  33.4 us (93%)
  local copies, waits for them, and re-layouts  1.36 us (4%)
  between operations  0.64 us (2%)
    pallas_call x1, Pallas kernels, on_device(): pl.pallas_call(functools.partial(kernel, tiles, chans, width), out_shape=...  33.4 us
    unnamed x2, local copies, waits for them, and re-layouts  1.36 us

profile of v5, /device:TPU:1, one launch (start us, length us, event | category | flops | bytes accessed | tf_op | source)
XLA Modules:
  0.0 35.4 jit_solution(14089949237434560436)
XLA Ops:
  0.6 33.4 %shard_map.68 = (bf16[64,2048]{1,0:T(8,128)(2,1)S(1)}, f32[64,432]{1,0:T(8,128)S(1)}) custom-call(bf16[32,1024]{1,0:T(8,128)(2,1)} %pts_ref.1, s32[1,1024]{1,0:T(1,128)} %bitcast.4, s32[1,1024]{1,0:T(1,128)} %bitcast.5, bf16[27,64,128]{2,1,0:T(8,128)(2,1)} %bitcast.3, bf16[64,2048]{1,0:T(8,128)(2,1)} %grad_ref.1), custom_call_target="tpu_custom_call" | custom-call | tf_op jit(solution)/shard_map/pallas_call | solution.py:407
  34.0 0.7 %copy.9 = bf16[64,2048]{1,0:T(8,128)(2,1)} copy(bf16[64,2048]{1,0:T(8,128)(2,1)S(1)} %get-tuple-element.4) | data formatting | bytes 524288
  34.7 0.7 %copy.10 = f32[64,432]{1,0:T(8,128)} copy(f32[64,432]{1,0:T(8,128)S(1)} %get-tuple-element.5) | data formatting | bytes 221184

commit v6 on v5

--- a/solution.py
+++ b/solution.py
@@ -52,6 +52,7 @@
     masked,
     partial,
     total,
+    blocks,
     handing,
     handed,
     sending,
@@ -313,15 +314,17 @@
                     total[:, place] += piece
     total[:, 27 * channels :] = jnp.zeros((outs, total.shape[1] - 27 * channels), jnp.float32)
 
-    def block(owner):
-        first = owner * width
-        base = pl.multiple_of(first // 128 * 128, 128)
-        window = total[:, pl.ds(base, span + 128)]
-        return pltpu.roll(window, span + 128 - lax.rem(first, 128), 1)[:, :span]
+    for owner in range(tiles):
+        base, skip = owner * width // 128 * 128, owner * width % 128
+        window = total[:, base : base + span + 128]
+        if skip:
+            window = pltpu.roll(window, span + 128 - skip, 1)
+        blocks[owner] = window[:, :span]
+        handing[owner] = window[:, :span].astype(jnp.bfloat16)
 
     def hand_copy(step):
         return pltpu.make_async_remote_copy(
-            src_ref=handing.at[step],
+            src_ref=handing.at[2 * chip_peer(step) + 1 - core],
             dst_ref=handed.at[step],
             send_sem=hand_send.at[step],
             recv_sem=hand_recv.at[step],
@@ -337,18 +340,15 @@
             device_id={"tile": 2 * chip_peer(step) + core},
         )
 
-    def hand_grads(step):
-        handing[step] = block(2 * chip_peer(step) + 1 - core)
-        hand_copy(step).start()
+    repeat(1, chips, lambda step: hand_copy(step).start())
+    hand_copy(0).start()
 
     def send_grads(step):
-        own = block(2 * chip_peer(step) + core)
         hand_copy(step).wait_recv()
-        sending[step] = (own + handed[step]).astype(jnp.bfloat16)
+        both = blocks[2 * chip_peer(step) + core] + handed[step].astype(jnp.float32)
+        sending[step] = both.astype(jnp.bfloat16)
         grad_copy(step).start()
 
-    repeat(1, chips, hand_grads)
-    hand_grads(0)
     repeat(1, chips, send_grads)
     for plane in range(DEPTH - LATE, DEPTH):
         forward(plane, columns_of(plane))
@@ -363,9 +363,8 @@
             output * occupied[plane : plane + 1, :]
         ).astype(jnp.bfloat16)
 
-    own_block = block(me)
     hand_copy(0).wait_recv()
-    total[:, :span] = own_block + handed[0]
+    total[:, :span] = blocks[me] + handed[0].astype(jnp.float32)
 
     def take_grads(step):
         grad_copy(step).wait_recv()
@@ -428,8 +427,9 @@
             pltpu.VMEM((DEPTH + 2, outs, PLANE), jnp.bfloat16),
             pltpu.VMEM((DEPTH, 3 * outs, PLANE), jnp.float32),
             pltpu.VMEM((outs, total_width), jnp.float32),
-            pltpu.VMEM((chips, outs, span), jnp.float32),
-            pltpu.VMEM((chips, outs, span), jnp.float32),
+            pltpu.VMEM((tiles, outs, span), jnp.float32),
+            pltpu.VMEM((tiles, outs, span), jnp.bfloat16),
+            pltpu.VMEM((chips, outs, span), jnp.bfloat16),
             pltpu.VMEM((chips, outs, span), jnp.bfloat16),
             pltpu.VMEM((chips, outs, span), jnp.bfloat16),
             dma((5,)),

time: 35.9 us -> 35.2 us (0.981)
  Pallas kernels: 33.4 us -> 32.8 us
    pallas_call x1, Pallas kernels: 33.4 us -> 32.8 us  [on_device(): pl.pallas_call(functools.partial(kernel, tiles, chans, width), out_shape=...]
where the time goes in v6:
time: 35.2 us; the launch traced here: 34.8 us
  Pallas kernels  32.8 us (93%)
  local copies, waits for them, and re-layouts  1.36 us (4%)
  between operations  0.64 us (2%)
    pallas_call x1, Pallas kernels, on_device(): pl.pallas_call(functools.partial(kernel, tiles, chans, width), out_shape=...  32.8 us
    unnamed x2, local copies, waits for them, and re-layouts  1.36 us

profile of v6, /device:TPU:1, one launch (start us, length us, event | category | flops | bytes accessed | tf_op | source)
XLA Modules:
  0.0 34.8 jit_solution(1294387812392126374)
XLA Ops:
  0.6 32.8 %shard_map.68 = (bf16[64,2048]{1,0:T(8,128)(2,1)S(1)}, f32[64,432]{1,0:T(8,128)S(1)}) custom-call(bf16[32,1024]{1,0:T(8,128)(2,1)} %pts_ref.1, s32[1,1024]{1,0:T(1,128)} %bitcast.4, s32[1,1024]{1,0:T(1,128)} %bitcast.5, bf16[27,64,128]{2,1,0:T(8,128)(2,1)} %bitcast.3, bf16[64,2048]{1,0:T(8,128)(2,1)} %grad_ref.1), custom_call_target="tpu_custom_call" | custom-call | tf_op jit(solution)/shard_map/pallas_call | solution.py:406
  33.5 0.7 %copy.9 = bf16[64,2048]{1,0:T(8,128)(2,1)} copy(bf16[64,2048]{1,0:T(8,128)(2,1)S(1)} %get-tuple-element.4) | data formatting | bytes 524288
  34.2 0.7 %copy.10 = f32[64,432]{1,0:T(8,128)} copy(f32[64,432]{1,0:T(8,128)S(1)} %get-tuple-element.5) | data formatting | bytes 221184

commit v7 on v6

--- a/solution.py
+++ b/solution.py
@@ -152,8 +152,8 @@
             device_id={"tile": sibling},
         )
 
+    repeat(1, tiles, lambda step: code_copy(step).start())
     repeat(1, chips, lambda step: pts_copy(step).start())
-    repeat(1, tiles, lambda step: code_copy(step).start())
     fetched[2].wait()
     share_copy(0).start()
 
@@ -195,12 +195,15 @@
         share_copy(step).wait_recv()
         take_points(2 * chip_giver(step) + 1 - core)
 
-    def take_sent(step):
+    def pass_points(step):
         pts_copy(step).wait_recv()
         share_copy(step).start()
+
+    def take_sent(step):
         take_points(2 * chip_giver(step) + core)
 
     take_shared(0)
+    repeat(1, chips, pass_points)
     repeat(1, chips, take_sent)
     repeat(1, chips, take_shared)
 

time: 35.2 us -> 34.5 us (0.980)
  Pallas kernels: 32.8 us -> 32.2 us
    pallas_call x1, Pallas kernels: 32.8 us -> 32.2 us  [on_device(): pl.pallas_call(functools.partial(kernel, tiles, chans, width), out_shape=...]
where the time goes in v7:
time: 34.5 us; the launch traced here: 34.2 us
  Pallas kernels  32.2 us (93%)
  local copies, waits for them, and re-layouts  1.36 us (4%)
  between operations  0.64 us (2%)
    pallas_call x1, Pallas kernels, on_device(): pl.pallas_call(functools.partial(kernel, tiles, chans, width), out_shape=...  32.2 us
    unnamed x2, local copies, waits for them, and re-layouts  1.36 us

profile of v7, /device:TPU:1, one launch (start us, length us, event | category | flops | bytes accessed | tf_op | source)
XLA Modules:
  0.0 34.2 jit_solution(15561077511186504675)
XLA Ops:
  0.6 32.2 %shard_map.68 = (bf16[64,2048]{1,0:T(8,128)(2,1)S(1)}, f32[64,432]{1,0:T(8,128)S(1)}) custom-call(bf16[32,1024]{1,0:T(8,128)(2,1)} %pts_ref.1, s32[1,1024]{1,0:T(1,128)} %bitcast.4, s32[1,1024]{1,0:T(1,128)} %bitcast.5, bf16[27,64,128]{2,1,0:T(8,128)(2,1)} %bitcast.3, bf16[64,2048]{1,0:T(8,128)(2,1)} %grad_ref.1), custom_call_target="tpu_custom_call" | custom-call | tf_op jit(solution)/shard_map/pallas_call | solution.py:409
  32.9 0.7 %copy.9 = bf16[64,2048]{1,0:T(8,128)(2,1)} copy(bf16[64,2048]{1,0:T(8,128)(2,1)S(1)} %get-tuple-element.4) | data formatting | bytes 524288
  33.6 0.7 %copy.10 = f32[64,432]{1,0:T(8,128)} copy(f32[64,432]{1,0:T(8,128)S(1)} %get-tuple-element.5) | data formatting | bytes 221184

commit v8 on v7

--- a/solution.py
+++ b/solution.py
@@ -13,7 +13,7 @@
 VOX = DEPTH * PLANE
 PADDED = PLANE + 2 * EDGE
 CHUNKS = 8
-LATE = 6
+LATE = 8
 PER_CHUNK = DEPTH // CHUNKS
 ROWS_MAJOR = (((1,), (1,)), ((), ()))
 

time: 34.5 us -> 34.5 us (level)
  no operation moved by 1% of the time
where the time goes in v8:
time: 34.5 us; the launch traced here: 34.2 us
  Pallas kernels  32.2 us (93%)
  local copies, waits for them, and re-layouts  1.36 us (4%)
  between operations  0.64 us (2%)
    pallas_call x1, Pallas kernels, on_device(): pl.pallas_call(functools.partial(kernel, tiles, chans, width), out_shape=...  32.2 us
    unnamed x2, local copies, waits for them, and re-layouts  1.36 us

profile of v8, /device:TPU:1, one launch (start us, length us, event | category | flops | bytes accessed | tf_op | source)
XLA Modules:
  0.0 34.2 jit_solution(2050314818826604744)
XLA Ops:
  0.6 32.2 %shard_map.68 = (bf16[64,2048]{1,0:T(8,128)(2,1)S(1)}, f32[64,432]{1,0:T(8,128)S(1)}) custom-call(bf16[32,1024]{1,0:T(8,128)(2,1)} %pts_ref.1, s32[1,1024]{1,0:T(1,128)} %bitcast.4, s32[1,1024]{1,0:T(1,128)} %bitcast.5, bf16[27,64,128]{2,1,0:T(8,128)(2,1)} %bitcast.3, bf16[64,2048]{1,0:T(8,128)(2,1)} %grad_ref.1), custom_call_target="tpu_custom_call" | custom-call | tf_op jit(solution)/shard_map/pallas_call | solution.py:409
  32.8 0.7 %copy.9 = bf16[64,2048]{1,0:T(8,128)(2,1)} copy(bf16[64,2048]{1,0:T(8,128)(2,1)S(1)} %get-tuple-element.4) | data formatting | bytes 524288
  33.5 0.7 %copy.10 = f32[64,432]{1,0:T(8,128)} copy(f32[64,432]{1,0:T(8,128)S(1)} %get-tuple-element.5) | data formatting | bytes 221184
